TPU v7x, 512 devices: a whole 4x4x16 slice. The times are simulated.
512 devices in a mesh: seq: 32 (over z, core), head: 4 (over x), dp: 4 (over y).
Axes of the slice: x: 4, y: 4, z: 16, core: 2. Of those that a mesh axis runs over, the one named last changes fastest.
Arguments:
- passthrough: bfloat16 [4, 8192, 1024], P('dp', 'seq', 'head'), may hold values from -6 to 6
- mixed_out: bfloat16 [4, 8192, 1024], P('dp', 'seq', 'head'), may hold values from -6 to 6
- grad_mixed: bfloat16 [4, 8192, 1024], P('dp', 'seq', 'head'), may hold values from -6 to 6
- grad_pass: bfloat16 [4, 8192, 1024], P('dp', 'seq', 'head'), may hold values from -6 to 6
- query_weight: bfloat16 [1024, 1024], P(None, 'head'), may hold values from -0.1875 to 0.1875
- key_weight: bfloat16 [1024, 1024], P(None, 'head'), may hold values from -0.1875 to 0.1875
- value_weight: bfloat16 [1024, 1024], P(None, 'head'), may hold values from -0.1875 to 0.1875
- random_features: bfloat16 [8, 128, 256], P('head'), may hold values from -5 to 5
- document_ids: int32 [4, 8192], P('dp', 'seq'), may hold values from 0 to 27, never falling along the last dimension, each value on 1 to 2048 neighbouring positions
Outputs:
- first_in: bfloat16 [4, 8192, 1024], P('dp', 'seq', 'head')
- grad_second: bfloat16 [4, 8192, 1024], P('dp', 'seq', 'head')
- grad_query_weight: float32 [1024, 1024], P(('seq', 'dp'), 'head')
- grad_key_weight: float32 [1024, 1024], P(('seq', 'dp'), 'head')
- grad_value_weight: float32 [1024, 1024], P(('seq', 'dp'), 'head')
Inputs may be any that keep to these rules, and one draw needn't show every extreme that they name: `document_ids`: along each context the number never falls; each of the 28 documents holds 1 to 2048 positions, and one holds exactly 2048.
All inputs are finite; a program needn't handle non-finite values.
Results may differ from a plain program's by a relative error of at most 0.018.
The roundings to bfloat16 on the way count: a program that leaves them out, or rounds other values in their place, can miss the bound.
Values may be sent and summed in bfloat16 or wider, within the bound.
A program may use at most 64 MiB of HBM per device.

v0:
```python
import jax
import jax.numpy as jnp
from jax import lax
from jax.sharding import PartitionSpec as P

EPSILON = 1e-06
HIGHEST = lax.Precision.HIGHEST


def carried_in(array, axis, join, neutral, backward):
    count = lax.axis_size(axis)
    place = lax.axis_index(axis)
    ahead = count - 1 - place if backward else place
    gathered = jax.tree.map(
        lambda a, kind: lax.all_gather(a.astype(kind), axis), array, (jnp.bfloat16, jnp.bfloat16)
    )
    state = jax.tree.map(lambda a, e: jnp.zeros_like(a) + jnp.asarray(e, a.dtype), array, neutral)

    def one(turn, state):
        source = count - 1 - turn if backward else turn
        return join(
            state,
            jax.tree.map(
                lambda a, own: lax.dynamic_index_in_dim(a, source, 0, False).astype(own.dtype),
                gathered,
                array,
            ),
        )

    return lax.fori_loop(0, ahead, one, state)


def to_heads(matrix, head_count):
    count_ctx, tok_rows, columns = matrix.shape
    return matrix.reshape(count_ctx, tok_rows, head_count, columns // head_count).transpose(
        0, 2, 1, 3
    )


def from_heads(tensor):
    count_ctx, head_count, tok_rows, head_dim = tensor.shape
    return tensor.transpose(0, 2, 1, 3).reshape(count_ctx, tok_rows, head_count * head_dim)


def feature_map(projected, random_features):
    head_dim = projected.shape[-1]
    mixing = jnp.einsum(
        "chtd,hdm->chtm", projected, random_features, preferred_element_type=jnp.float32
    )
    widened = projected.astype(jnp.float32)
    squares = jnp.sum(widened * widened, axis=-1, keepdims=True)
    exponent = mixing / head_dim**0.25 - squares / (2.0 * head_dim**0.5)
    return (jnp.exp(exponent) / random_features.shape[-1] ** 0.5).astype(jnp.bfloat16)


def feature_grad(dfeature, feature, projected, random_features):
    head_dim = projected.shape[-1]
    dexponent = dfeature * feature.astype(jnp.float32)
    rounded = dexponent.astype(jnp.bfloat16)
    back_proj = jnp.einsum(
        "chtm,hdm->chtd", rounded, random_features, preferred_element_type=jnp.float32
    )
    totals = jnp.sum(dexponent, axis=-1, keepdims=True)
    result = back_proj / head_dim**0.25 - projected.astype(jnp.float32) * totals / head_dim**0.5
    return result.astype(jnp.bfloat16)


def join_state(earlier, later_part):
    early_state, early_id = earlier
    late_state, late_id = later_part
    same_id = (early_id == late_id)[:, None, None, None]
    vacant = (late_id < 0.0)[:, None, None, None]
    merged = jnp.where(vacant, early_state, late_state + jnp.where(same_id, early_state, 0.0))
    new_id = jnp.where(late_id < 0.0, early_id, late_id)
    return (merged, new_id)


def shards(
    passthrough,
    mixed_out,
    grad_mixed,
    grad_pass,
    query_weight,
    key_weight,
    value_weight,
    random_features,
    document_ids,
):
    head_count = random_features.shape[0]
    count_ctx, tok_rows, local_width = passthrough.shape
    whole_in = lax.all_gather(passthrough, "head", axis=2, tiled=True)
    widened = whole_in.astype(jnp.float32)
    full_width = widened.shape[2]
    inv_rms = lax.rsqrt(jnp.mean(widened * widened, axis=2, keepdims=True) + EPSILON)
    normed = (widened * inv_rms).astype(jnp.bfloat16)
    query_proj = jnp.einsum(
        "ctd,dj->ctj", normed, query_weight, preferred_element_type=jnp.float32
    ).astype(jnp.bfloat16)
    key_proj = jnp.einsum(
        "ctd,dj->ctj", normed, key_weight, preferred_element_type=jnp.float32
    ).astype(jnp.bfloat16)
    value_proj = jnp.einsum(
        "ctd,dj->ctj", normed, value_weight, preferred_element_type=jnp.float32
    ).astype(jnp.bfloat16)
    query_heads = to_heads(query_proj, head_count)
    key_heads = to_heads(key_proj, head_count)
    value_heads = to_heads(value_proj, head_count)
    feat_query = feature_map(query_heads, random_features)
    feat_key = feature_map(key_heads, random_features)
    ids_wide = document_ids.astype(jnp.float32)
    rows_idx = lax.broadcasted_iota(jnp.int32, (tok_rows, tok_rows), 0)
    cols_idx = lax.broadcasted_iota(jnp.int32, (tok_rows, tok_rows), 1)
    same_doc = document_ids[:, :, None] == document_ids[:, None, :]
    allowed = (same_doc & (rows_idx >= cols_idx)[None])[:, None]
    scores = jnp.einsum("chtm,chsm->chts", feat_query, feat_key, preferred_element_type=jnp.float32)
    pair_weight = jnp.where(allowed, scores, 0.0).astype(jnp.bfloat16)
    attn_local = jnp.einsum(
        "chts,chsd->chtd", pair_weight, value_heads, preferred_element_type=jnp.float32
    )
    last_ids = ids_wide[:, -1]
    tail_mask = (ids_wide == last_ids[:, None])[:, None, :, None]
    tail_keys = jnp.where(tail_mask, feat_key, jnp.zeros_like(feat_key))
    tail_state = jnp.einsum(
        "chtm,chtd->chmd", tail_keys, value_heads, preferred_element_type=jnp.float32
    )
    empty_state = (jnp.zeros_like(tail_state), jnp.full_like(last_ids, -1.0))
    state_in, state_id = carried_in((tail_state, last_ids), "seq", join_state, empty_state, False)
    head_on = (ids_wide == state_id[:, None])[:, None, :, None]
    fq_wide = feat_query.astype(jnp.float32)
    carried = jnp.einsum("chtm,chmd->chtd", fq_wide, state_in, precision=HIGHEST)
    attention = attn_local + jnp.where(head_on, carried, 0.0)
    inv_attn = lax.rsqrt(jnp.mean(attention * attention, axis=-1, keepdims=True) + EPSILON)
    act = attention * inv_attn
    first_in = (mixed_out.astype(jnp.float32) - from_heads(act)).astype(jnp.bfloat16)
    grad_act = to_heads(grad_mixed, head_count).astype(jnp.float32)
    grad_attn = (
        inv_attn * (grad_act - act * jnp.mean(grad_act * act, axis=-1, keepdims=True))
    ).astype(jnp.bfloat16)
    dscores = jnp.einsum(
        "chtd,chsd->chts", grad_attn, value_heads, preferred_element_type=jnp.float32
    )
    dpair = jnp.where(allowed, dscores, 0.0).astype(jnp.bfloat16)
    first_ids = ids_wide[:, 0]
    head_mask = (ids_wide == first_ids[:, None])[:, None, :, None]
    head_query = jnp.where(head_mask, feat_query, jnp.zeros_like(feat_query))
    head_state = jnp.einsum(
        "chtm,chtd->chmd", head_query, grad_attn, preferred_element_type=jnp.float32
    )
    state_later, later_id = carried_in(
        (head_state, first_ids), "seq", join_state, empty_state, True
    )
    tail_on = (ids_wide == later_id[:, None])[:, None, :, None]
    grad_wide = grad_attn.astype(jnp.float32)
    dfeat_query = jnp.einsum("chts,chsm->chtm", dpair, feat_key, preferred_element_type=jnp.float32)
    dfeat_query = dfeat_query + jnp.where(
        head_on, jnp.einsum("chtd,chmd->chtm", grad_wide, state_in, precision=HIGHEST), 0.0
    )
    dfeat_key = jnp.einsum("chts,chtm->chsm", dpair, feat_query, preferred_element_type=jnp.float32)
    dfeat_key = dfeat_key + jnp.where(
        tail_on,
        jnp.einsum(
            "chsd,chmd->chsm", value_heads.astype(jnp.float32), state_later, precision=HIGHEST
        ),
        0.0,
    )
    dvalue = jnp.einsum(
        "chts,chtd->chsd", pair_weight, grad_attn, preferred_element_type=jnp.float32
    )
    dvalue = dvalue + jnp.where(
        tail_on,
        jnp.einsum("chsm,chmd->chsd", feat_key.astype(jnp.float32), state_later, precision=HIGHEST),
        0.0,
    )
    dvalue = dvalue.astype(jnp.bfloat16)
    dquery = feature_grad(dfeat_query, feat_query, query_heads, random_features)
    dkey = feature_grad(dfeat_key, feat_key, key_heads, random_features)
    grads_flat = jnp.concatenate([from_heads(dquery), from_heads(dkey), from_heads(dvalue)], axis=2)
    weights_all = jnp.concatenate([query_weight, key_weight, value_weight], axis=1)
    partial_value = jnp.einsum(
        "ctj,dj->ctd", grads_flat, weights_all, preferred_element_type=jnp.float32
    )
    grad_normed = lax.psum_scatter(
        partial_value.astype(jnp.bfloat16), "head", scatter_dimension=2, tiled=True
    ).astype(jnp.float32)
    norm_local = passthrough.astype(jnp.float32) * inv_rms
    dot_sum = lax.psum(jnp.sum(grad_normed * norm_local, axis=2), "head")
    grad_second = grad_pass.astype(jnp.float32) + inv_rms * (
        grad_normed - norm_local * (dot_sum / full_width)[:, :, None]
    )
    grad_second = grad_second.astype(jnp.bfloat16)
    seq_count = lax.axis_size("seq")
    dp_count = lax.axis_size("dp")
    total_rows = count_ctx * tok_rows * seq_count * dp_count
    grad_scale = 1.0 / total_rows**0.5
    summed = lax.psum_scatter(
        jnp.einsum("ctr,ctj->rj", normed, grads_flat, preferred_element_type=jnp.float32)
        * grad_scale,
        ("seq", "dp"),
        scatter_dimension=0,
        tiled=True,
    )
    return (
        first_in,
        grad_second,
        summed[:, :local_width],
        summed[:, local_width : 2 * local_width],
        summed[:, 2 * local_width :],
    )


def solution(mesh):
    placed = (
        P("dp", "seq", "head"),
        P("dp", "seq", "head"),
        P("dp", "seq", "head"),
        P("dp", "seq", "head"),
        P(None, "head"),
        P(None, "head"),
        P(None, "head"),
        P("head", None, None),
        P("dp", "seq"),
    )
    return jax.shard_map(
        shards,
        mesh=mesh,
        in_specs=placed,
        out_specs=(
            P("dp", "seq", "head"),
            P("dp", "seq", "head"),
            P(("seq", "dp"), "head"),
            P(("seq", "dp"), "head"),
            P(("seq", "dp"), "head"),
        ),
        check_vma=False,
    )
```

profile of v0, /device:TPU:2, one launch (start us, length us, event | category | flops | bytes accessed | tf_op | source)
XLA Modules:
  0.0 698.9 jit_solution(1416142091037650247)
XLA Ops:
  8.6 15.7 %all_gather.23 = bf16[1,256,1024]{2,1,0:T(8,128)(2,1)S(1)} all-gather(bf16[1,256,256]{2,1,0:T(8,128)(2,1)} %param.13), channel_id=1, replica_groups=mesh['seq'=32,'head'=4,'dp'=4] {'head'}, dimensions={2}, use_global_device_ids=true | all-gather | bytes 655360 | tf_op jit(solution)/shard_map/all_gather | solution.py:91
  24.6 1.5 convolution_convert_fusion.3
  26.1 1.5 convolution_convert_fusion.2
  27.7 1.3 compare_reduce_fusion.1
  31.7 1.3 dynamic-slice
  34.4 50.4 %all-reduce.2 = (bf16[32]{0:T(256)(128)(2,1)S(1)}, bf16[32]{0:T(256)(128)(2,1)S(1)}) all-reduce(bf16[32]{0:T(256)(128)(2,1)S(1)} %dynamic-update-slice, bf16[32]{0:T(256)(128)(2,1)S(1)} %dynamic-update-slice.1), channel_id=1, replica_groups=mesh['seq'=32,'head'=4,'dp'=4] {'seq'}, use_global_device_ids=true, to_apply=%add | all-reduce | flops 64 | bytes 256
  86.1 20.5 %all-gather.5.cloned.1.call-done = bf16[64,256,128]{2,1,0:T(8,128)(2,1)} async-done(((bf16[2,256,128]{2,1,0:T(8,128)(2,1)}), bf16[64,256,128]{2,1,0:T(8,128)(2,1)}) %all-gather.5.cloned.1.call-update) | async-done | bytes 4194320 | tf_op jit(solution)/shard_map/all_gather | solution.py:15
  110.0 177.3 %all-gather.7.cloned.1.call-done = bf16[64,256,128]{2,1,0:T(8,128)(2,1)} async-done(((bf16[2,256,128]{2,1,0:T(8,128)(2,1)}), bf16[64,256,128]{2,1,0:T(8,128)(2,1)}) %all-gather.7.cloned.1.call-update) | async-done | bytes 4194320 | tf_op jit(solution)/shard_map/all_gather | solution.py:15
  287.3 111.8 %while.27 = (s32[]{:T(128)}, f32[1,2,256,128]{3,2,1,0:T(8,128)S(1)}, f32[1]{0:T(128)}, s32[]{:T(128)}, bf16[32,1]{0,1:T(2,128)(2,1)S(1)}, /*index=5*/bf16[32,1,2...) while((s32[]{:T(128)}, ...), condition=%wide.region_9.10_spmd, body=%wide.region_8.9_spmd.sunk | while | flops 262153 | bytes 655570 | solution.py:30
  289.8 1.0 fusion.111
  293.4 1.0 fusion.111
  297.0 1.0 fusion.111
  300.6 1.0 fusion.111
  304.3 1.0 fusion.111
  307.9 1.0 fusion.111
  311.5 1.0 fusion.111
  315.1 1.0 fusion.111
  318.7 1.0 fusion.111
  322.3 1.0 fusion.111
  325.9 1.0 fusion.111
  329.5 1.0 fusion.111
  333.1 1.0 fusion.111
  336.7 1.0 fusion.111
  340.3 1.0 fusion.111
  343.9 1.0 fusion.111
  347.5 1.0 fusion.111
  351.2 1.0 fusion.111
  354.8 1.0 fusion.111
  358.4 1.0 fusion.111
  362.0 1.0 fusion.111
  365.6 1.0 fusion.111
  369.2 1.0 fusion.111
  372.8 1.0 fusion.111
  376.4 1.0 fusion.111
  380.0 1.0 fusion.111
  383.6 1.0 fusion.111
  387.2 1.0 fusion.111
  390.8 1.0 fusion.111
  394.4 1.0 fusion.111
  398.0 1.0 fusion.111
  400.2 2.8 fusion.11
  403.1 2.4 convolution_multiply_fusion
  406.4 15.4 %reduce-scatter.3.cloned.1.call-done = bf16[1,256,256]{2,1,0:T(8,128)(2,1)} async-done(((bf16[1,256,1024]{2,1,0:T(8,128)(2,1)}), bf16[1,256,256]{2,1,0:T(8,128)(2,1)}) %reduce-scatter.3.cloned.1.call-update) | async-done | bytes 131088 | tf_op jit(solution)/shard_map/reduce_scatter | solution.py:182
  421.8 1.1 fusion.43
  422.9 9.7 %psum.7 = f32[1,256]{1,0:T(1,128)S(1)} all-reduce(f32[1,256]{1,0:T(1,128)S(1)} %bitcast.261), channel_id=1, replica_groups=mesh['seq'=32,'head'=4,'dp'=4] {'head'}, use_global_device_ids=true, to_apply=%region_13.14 | all-reduce | flops 256 | bytes 2048 | tf_op jit(solution)/shard_map/psum | solution.py:186
  432.6 1.7 fusion.46
  434.3 256.8 %reduce-scatter.5.cloned.1.call-done = f32[8,768]{1,0:T(8,128)} async-done(((f32[1024,768]{1,0:T(8,128)}), f32[8,768]{1,0:T(8,128)}) %reduce-scatter.5.cloned.1.call-update) | async-done | bytes 24592 | tf_op jit(solution)/shard_map/reduce_scatter | solution.py:195
  691.1 1.3 fusion.85
  (97 shorter events, 29.3 us)
Async XLA Ops:
  7.2 21.8 %copy-start = (bf16[2,128,256]{2,1,0:T(8,128)(2,1)S(1)}, bf16[2,128,256]{2,1,0:T(8,128)(2,1)}, u32[]{:S(2)}) copy-start(bf16[2,128,256]{2,1,0:T(8,128)(2,1)} %param.20) | copy-start | bytes 393220
  7.2 20.5 %copy-start.5 = (s32[1,256]{1,0:T(1,128)S(1)}, s32[1,256]{1,0:T(1,128)}, u32[]{:S(2)}) copy-start(s32[1,256]{1,0:T(1,128)} %param.21) | copy-start | bytes 3076
  7.2 24.4 %copy-start.2 = (bf16[1,256,256]{2,1,0:T(8,128)(2,1)S(1)}, bf16[1,256,256]{2,1,0:T(8,128)(2,1)}, u32[]{:S(2)}) copy-start(bf16[1,256,256]{2,1,0:T(8,128)(2,1)} %param.15) | copy-start | bytes 393220
  7.2 77.7 %copy-start.6 = (bf16[1024,256]{1,0:T(8,128)(2,1)S(1)}, bf16[1024,256]{1,0:T(8,128)(2,1)}, u32[]{:S(2)}) copy-start(bf16[1024,256]{1,0:T(8,128)(2,1)} %param.17) | copy-start | bytes 1572868
  7.2 99.4 %all-gather.5.cloned.1.call-start = ((), (), s32[]{:S(2)}) async-start(), calls=%async_computation.4 | async-start | bytes 4325376 | tf_op jit(solution)/shard_map/all_gather | solution.py:15
  30.2 257.0 %all-gather.7.cloned.1.call-start = ((), (), s32[]{:S(2)}) async-start(), calls=%async_computation.5 | async-start | bytes 4325376 | tf_op jit(solution)/shard_map/all_gather | solution.py:15
  108.3 313.4 %reduce-scatter.3.cloned.1.call-start = ((), (), s32[]{:S(2)}) async-start(), calls=%async_computation.2 | async-start | bytes 655360 | tf_op jit(solution)/shard_map/reduce_scatter | solution.py:182
  403.0 2.6 copy-start.3
  403.1 18.7 %copy-start.1 = (bf16[1,256,256]{2,1,0:T(8,128)(2,1)S(1)}, bf16[1,256,256]{2,1,0:T(8,128)(2,1)}, u32[]{:S(2)}) copy-start(bf16[1,256,256]{2,1,0:T(8,128)(2,1)} %param.13) | copy-start | bytes 393220
  403.1 288.0 %reduce-scatter.5.cloned.1.call-start = ((), (), s32[]{:S(2)}) async-start(), calls=%async_computation.3 | async-start | bytes 3170304 | tf_op jit(solution)/shard_map/reduce_scatter | solution.py:195
  405.5 27.1 %copy-start.4 = (bf16[1,256,256]{2,1,0:T(8,128)(2,1)S(1)}, bf16[1,256,256]{2,1,0:T(8,128)(2,1)}, u32[]{:S(2)}) copy-start(bf16[1,256,256]{2,1,0:T(8,128)(2,1)} %param.16) | copy-start | bytes 393220
Sparse Core Ops, SparseCore 0:
  30.3 76.2 all-gather.4
  109.3 177.9 all-gather.6
  403.2 18.5 reduce-scatter.2
  426.3 264.7 reduce-scatter.4
where the time goes:
time: 701 us; the launch traced here: 699 us
  waiting for transfers between devices  470 us (67%)
  blocking collectives  75.9 us (11%)
  loops' own time  61.4 us (9%)
  other arithmetic  38.4 us (5%)
  local copies, waits for them, and re-layouts  23.3 us (3%)
  between operations  15.4 us (2%)
  matrix products  14.5 us (2%)
    reduce_scatter x1, waiting for transfers between devices, shards(): lax.psum_scatter(jnp.einsum('ctr,ctj->rj', normed, grads_flat, preferred_...  257 us
    all_gather x2, waiting for transfers between devices, carried_in(): lax.all_gather(a.astype(kind), axis)  198 us
    another operation x2, loops' own time, carried_in(): return lax.fori_loop(0, ahead, one, state)  61.4 us
    unnamed x1, blocking collectives  50.4 us
    select_n x31, other arithmetic, join_state(): jnp.where(vacant, early_state, late_state + jnp.where(same_id, early_stat...  32.2 us
    dynamic_slice x31, local copies, waits for them, and re-layouts, one(): lax.dynamic_index_in_dim(a, source, 0, False).astype(own.dtype)  18.2 us
    all_gather x1, blocking collectives, shards(): whole_in = lax.all_gather(passthrough, 'head', axis=2, tiled=True)  15.7 us
    reduce_scatter x1, waiting for transfers between devices, shards(): lax.psum_scatter(partial_value.astype(jnp.bfloat16), 'head', scatter_dime...  15.4 us
  transfers between devices with their start and end apart: 4, of which 4 were waited for; matrix products, arithmetic and copies ran while one was open for 2% of the time, Pallas kernels for 0%

commit v1 on v0

--- a/solution.py
+++ b/solution.py
@@ -88,7 +88,9 @@
 ):
     head_count = random_features.shape[0]
     count_ctx, tok_rows, local_width = passthrough.shape
-    whole_in = lax.all_gather(passthrough, "head", axis=2, tiled=True)
+    whole_in = jnp.concatenate(
+        lax.all_to_all(jnp.stack([passthrough] * lax.axis_size("head")), "head", 0, 0), axis=2
+    )
     widened = whole_in.astype(jnp.float32)
     full_width = widened.shape[2]
     inv_rms = lax.rsqrt(jnp.mean(widened * widened, axis=2, keepdims=True) + EPSILON)

time: 701 us -> 696 us (level)
  blocking collectives: 75.9 us -> 61.5 us
  starting transfers between devices: 0.16 us -> 9.6 us
    all_gather x1 -> x0, blocking collectives: 15.7 us -> none  [shards(): whole_in = lax.all_gather(passthrough, 'head', axis=2, tiled=True)]
    all_to_all x0 -> x1, starting transfers between devices: none -> 9.48 us  [shards(): lax.all_to_all(jnp.stack([passthrough] * lax.axis_size('head')), 'head',...]
  transfers between devices with their start and end apart: 4 -> 5, of which waited for: 4 -> 5; matrix products, arithmetic and copies ran while one was open for 2% -> 2% of each run, Pallas kernels for 0% -> 0%
where the time goes in v1:
time: 696 us; the launch traced here: 695 us
  waiting for transfers between devices  469 us (67%)
  blocking collectives  61.5 us (9%)
  loops' own time  61.4 us (9%)
  other arithmetic  39 us (6%)
  local copies, waits for them, and re-layouts  26.2 us (4%)
  between operations  15.4 us (2%)
  matrix products  12 us (2%)
  starting transfers between devices  9.6 us (1%)
    reduce_scatter x1, waiting for transfers between devices, shards(): lax.psum_scatter(jnp.einsum('ctr,ctj->rj', normed, grads_flat, preferred_...  257 us
    all_gather x2, waiting for transfers between devices, carried_in(): lax.all_gather(a.astype(kind), axis)  194 us
    another operation x2, loops' own time, carried_in(): return lax.fori_loop(0, ahead, one, state)  61.4 us
    unnamed x1, blocking collectives  51.8 us
    select_n x31, other arithmetic, join_state(): jnp.where(vacant, early_state, late_state + jnp.where(same_id, early_stat...  32.2 us
    dynamic_slice x31, local copies, waits for them, and re-layouts, one(): lax.dynamic_index_in_dim(a, source, 0, False).astype(own.dtype)  18.2 us
    reduce_scatter x1, waiting for transfers between devices, shards(): lax.psum_scatter(partial_value.astype(jnp.bfloat16), 'head', scatter_dime...  15.5 us
  transfers between devices with their start and end apart: 5, of which 5 were waited for; matrix products, arithmetic and copies ran while one was open for 2% of the time, Pallas kernels for 0%

profile of v1, /device:TPU:2, one launch (start us, length us, event | category | flops | bytes accessed | tf_op | source)
XLA Modules:
  0.0 694.6 jit_solution(11806769577624319898)
XLA Ops:
  7.2 1.1 copy.70
  9.1 9.5 %all-to-all-start = ((bf16[4,1,256,256]{2,3,1,0:T(8,128)(2,1)}), bf16[4,1,256,256]{2,3,1,0:T(8,128)(2,1)S(1)}, u32[]{:S(2)}, u32[]{:S(2)}) async-start(bf16[4,1,256,256]{2,3,1,0:T(8,128)(2,1)} %stack.2), calls=%async_computation | async-start | bytes 1048576 | tf_op jit(solution)/shard_map/all_to_all | solution.py:92
  19.8 2.0 compare_reduce_fusion.1
  21.8 3.4 all-to-all-done
  30.1 1.3 dynamic-slice
  32.9 51.8 %all-reduce.2 = (bf16[32]{0:T(256)(128)(2,1)S(1)}, bf16[32]{0:T(256)(128)(2,1)}) all-reduce(bf16[32]{0:T(256)(128)(2,1)S(1)} %dynamic-update-slice, bf16[32]{0:T(256)(128)(2,1)S(1)} %dynamic-update-slice.1), channel_id=1, replica_groups=mesh['seq'=32,'head'=4,'dp'=4] {'seq'}, use_global_device_ids=true, to_apply=%add | all-reduce | flops 64 | bytes 256
  85.8 16.4 %all-gather.5.cloned.1.call-done = bf16[64,256,128]{2,1,0:T(8,128)(2,1)} async-done(((bf16[2,256,128]{2,1,0:T(8,128)(2,1)}), bf16[64,256,128]{2,1,0:T(8,128)(2,1)}) %all-gather.5.cloned.1.call-update) | async-done | bytes 4194320 | tf_op jit(solution)/shard_map/all_gather | solution.py:15
  105.6 177.3 %all-gather.7.cloned.1.call-done = bf16[64,256,128]{2,1,0:T(8,128)(2,1)} async-done(((bf16[2,256,128]{2,1,0:T(8,128)(2,1)}), bf16[64,256,128]{2,1,0:T(8,128)(2,1)}) %all-gather.7.cloned.1.call-update) | async-done | bytes 4194320 | tf_op jit(solution)/shard_map/all_gather | solution.py:15
  283.0 111.8 %while.27 = (s32[]{:T(128)}, f32[1,2,256,128]{3,2,1,0:T(8,128)S(1)}, f32[1]{0:T(128)}, s32[]{:T(128)}, bf16[32,1]{0,1:T(2,128)(2,1)S(1)}, /*index=5*/bf16[32,1,2...) while((s32[]{:T(128)}, ...), condition=%wide.region_9.10_spmd, body=%wide.region_8.9_spmd.sunk | while | flops 262153 | bytes 655570 | solution.py:30
  285.6 1.0 fusion.111
  289.2 1.0 fusion.111
  292.8 1.0 fusion.111
  296.4 1.0 fusion.111
  300.0 1.0 fusion.111
  303.6 1.0 fusion.111
  307.2 1.0 fusion.111
  310.8 1.0 fusion.111
  314.4 1.0 fusion.111
  318.0 1.0 fusion.111
  321.6 1.0 fusion.111
  325.2 1.0 fusion.111
  328.8 1.0 fusion.111
  332.4 1.0 fusion.111
  336.0 1.0 fusion.111
  339.6 1.0 fusion.111
  343.2 1.0 fusion.111
  346.8 1.0 fusion.111
  350.5 1.0 fusion.111
  354.1 1.0 fusion.111
  357.7 1.0 fusion.111
  361.3 1.0 fusion.111
  364.9 1.0 fusion.111
  368.5 1.0 fusion.111
  372.1 1.0 fusion.111
  375.7 1.0 fusion.111
  379.3 1.0 fusion.111
  382.9 1.0 fusion.111
  386.5 1.0 fusion.111
  390.1 1.0 fusion.111
  393.7 1.0 fusion.111
  395.9 2.8 fusion.11
  398.7 2.3 convolution_multiply_fusion
  401.9 15.5 %reduce-scatter.3.cloned.1.call-done = bf16[1,256,256]{2,1,0:T(8,128)(2,1)} async-done(((bf16[1,256,1024]{2,1,0:T(8,128)(2,1)}), bf16[1,256,256]{2,1,0:T(8,128)(2,1)}) %reduce-scatter.3.cloned.1.call-update) | async-done | bytes 131088 | tf_op jit(solution)/shard_map/reduce_scatter | solution.py:184
  417.4 1.1 fusion.44
  418.5 9.7 %psum.7 = f32[1,256]{1,0:T(1,128)S(1)} all-reduce(f32[1,256]{1,0:T(1,128)S(1)} %bitcast.277), channel_id=1, replica_groups=mesh['seq'=32,'head'=4,'dp'=4] {'head'}, use_global_device_ids=true, to_apply=%region_13.14 | all-reduce | flops 256 | bytes 2048 | tf_op jit(solution)/shard_map/psum | solution.py:188
  428.3 1.7 fusion.47
  430.0 256.7 %reduce-scatter.5.cloned.1.call-done = f32[8,768]{1,0:T(8,128)} async-done(((f32[1024,768]{1,0:T(8,128)}), f32[8,768]{1,0:T(8,128)}) %reduce-scatter.5.cloned.1.call-update) | async-done | bytes 24592 | tf_op jit(solution)/shard_map/reduce_scatter | solution.py:197
  686.7 1.3 fusion.82
  (114 shorter events, 31.7 us)
Async XLA Ops:
  7.2 19.4 %copy-start = (bf16[2,128,256]{2,1,0:T(8,128)(2,1)S(1)}, bf16[2,128,256]{2,1,0:T(8,128)(2,1)}, u32[]{:S(2)}) copy-start(bf16[2,128,256]{2,1,0:T(8,128)(2,1)} %param.20) | copy-start | bytes 393220
  7.2 18.4 %copy-start.2 = (bf16[1024,256]{1,0:T(8,128)(2,1)S(1)}, bf16[1024,256]{1,0:T(8,128)(2,1)}, u32[]{:S(2)}) copy-start(bf16[1024,256]{1,0:T(8,128)(2,1)} %param.18) | copy-start | bytes 1572868
  9.1 16.9 %copy-start.3 = (bf16[1024,256]{1,0:T(8,128)(2,1)S(1)}, bf16[1024,256]{1,0:T(8,128)(2,1)}, u32[]{:S(2)}) copy-start(bf16[1024,256]{1,0:T(8,128)(2,1)} %param.19) | copy-start | bytes 1572868
  9.1 16.1 %all-to-all-start = ((bf16[4,1,256,256]{2,3,1,0:T(8,128)(2,1)}), bf16[4,1,256,256]{2,3,1,0:T(8,128)(2,1)S(1)}, u32[]{:S(2)}, u32[]{:S(2)}) async-start(bf16[4,1,256,256]{2,3,1,0:T(8,128)(2,1)} %stack.2), calls=%async_computation | async-start | bytes 1048576 | tf_op jit(solution)/shard_map/all_to_all | solution.py:92
  18.6 83.6 %all-gather.5.cloned.1.call-start = ((), (), s32[]{:S(2)}) async-start(), calls=%async_computation.5 | async-start | bytes 4325376 | tf_op jit(solution)/shard_map/all_gather | solution.py:15
  25.5 59.2 %copy-start.11 = (s32[1,256]{1,0:T(1,128)S(1)}, s32[1,256]{1,0:T(1,128)}, u32[]{:S(2)}) copy-start(s32[1,256]{1,0:T(1,128)} %param.21) | copy-start | bytes 3076
  25.5 59.3 %copy-start.4 = (bf16[1024,256]{1,0:T(8,128)(2,1)S(1)}, bf16[1024,256]{1,0:T(8,128)(2,1)}, u32[]{:S(2)}) copy-start(bf16[1024,256]{1,0:T(8,128)(2,1)} %param.17) | copy-start | bytes 1572868
  26.5 75.7 %copy-start.5 = (bf16[1,256,2,128]{3,1,2,0:T(8,128)(2,1)}, bf16[1,256,2,128]{3,1,2,0:T(8,128)(2,1)S(1)}, u32[]{:S(2)}) copy-start(bf16[1,256,2,128]{3,1,2,0:T(8,128)(2,1)S(1)} %copy.79) | copy-start | bytes 393220
  27.7 255.2 %all-gather.7.cloned.1.call-start = ((), (), s32[]{:S(2)}) async-start(), calls=%async_computation.6 | async-start | bytes 4325376 | tf_op jit(solution)/shard_map/all_gather | solution.py:15
  84.8 0.7 copy-start.9
  102.2 1.8 copy-start.10
  102.2 1.8 copy-start.6
  103.9 179.0 %copy-start.12 = (bf16[32]{0:T(256)(128)(2,1)S(1)}, bf16[32]{0:T(256)(128)(2,1)}, u32[]{:S(2)}) copy-start(bf16[32]{0:T(256)(128)(2,1)} %get-tuple-element.187) | copy-start | bytes 196
  104.0 313.5 %reduce-scatter.3.cloned.1.call-start = ((), (), s32[]{:S(2)}) async-start(), calls=%async_computation.3 | async-start | bytes 655360 | tf_op jit(solution)/shard_map/reduce_scatter | solution.py:184
  398.7 288.0 %reduce-scatter.5.cloned.1.call-start = ((), (), s32[]{:S(2)}) async-start(), calls=%async_computation.4 | async-start | bytes 3170304 | tf_op jit(solution)/shard_map/reduce_scatter | solution.py:197
  398.7 2.5 copy-start.7
  401.0 16.4 %copy-start.1 = (bf16[1,256,256]{2,1,0:T(8,128)(2,1)S(1)}, bf16[1,256,256]{2,1,0:T(8,128)(2,1)}, u32[]{:S(2)}) copy-start(bf16[1,256,256]{2,1,0:T(8,128)(2,1)} %param.13) | copy-start | bytes 393220
  401.0 27.2 %copy-start.8 = (bf16[1,256,256]{2,1,0:T(8,128)(2,1)S(1)}, bf16[1,256,256]{2,1,0:T(8,128)(2,1)}, u32[]{:S(2)}) copy-start(bf16[1,256,256]{2,1,0:T(8,128)(2,1)} %param.16) | copy-start | bytes 393220
Sparse Core Ops, SparseCore 0:
  27.9 74.2 all-gather.4
  104.9 178.0 all-gather.6
  398.8 18.5 reduce-scatter.2
  421.9 264.7 reduce-scatter.4
